TPU v7x, 128 devices: a whole 4x4x4 slice. The times are simulated.
128 devices in a mesh: ctx: 16 (over y, z), mdl: 8 (over x, core).
Axes of the slice: x: 4, y: 4, z: 4, core: 2. Of those that a mesh axis runs over, the one named last changes fastest.
Arguments:
- queries: bfloat16 [2048, 8192], P('ctx', 'mdl'), may hold values from -6 to 6
- keys: bfloat16 [2048, 8192], P('ctx', 'mdl'), may hold values from -6 to 6
- values: bfloat16 [2048, 8192], P('ctx', 'mdl'), may hold values from -6 to 6
- prefix_state: float32 [64, 128, 128], P('mdl'), may hold values from -64 to 64
- out_gain: bfloat16 [8192], P('mdl'), may hold values from 0.099609375 to 1.8984375
- out_weight: bfloat16 [8192, 6144], P('mdl', 'ctx'), may hold values from -0.0625 to 0.0625
- resid: bfloat16 [2048, 6144], P('ctx', 'mdl'), may hold values from -6 to 6
- ffn_gain: bfloat16 [6144], replicated, may hold values from 0.099609375 to 1.8984375
- expert_ids: int32 [2048, 2], P('ctx'), may hold values from 0 to 7, all different within a row; in each aligned block of 128 rows (0 to 127, 128 to 255, ...) at most 48 rows name the same one
- route_weights: float32 [2048, 2], P('ctx'), may hold values from 0.1 to 1
- gate_weight: bfloat16 [8, 6144, 9216], P('mdl', None, 'ctx'), may hold values from -0.078125 to 0.078125
- up_weight: bfloat16 [8, 6144, 9216], P('mdl', None, 'ctx'), may hold values from -0.078125 to 0.078125
- down_weight: bfloat16 [8, 9216, 6144], P('mdl', 'ctx'), may hold values from -0.0625 to 0.0625
Outputs:
- layer_out: bfloat16 [2048, 6144], P('ctx', 'mdl')
Inputs may be any that keep to these rules, and one draw needn't show every extreme that they name: `expert_ids`: each row names 2 different experts. In each aligned block of 128 rows no expert is named by more than 48 rows, a bound that some block reaches.
All inputs are finite; a program needn't handle non-finite values.
Results may differ from a plain program's by a relative error of at most 0.024.
Values may be sent and summed in bfloat16 or wider, within the bound.
No kernel may reach another device: no remote copies, remote signals or barrier semaphores. Data moves between devices by JAX's collectives and lax.ppermute only.
A program may use at most 128 MiB of HBM per device.

v0:
```python
import jax
import jax.numpy as jnp
from jax import lax
from jax.sharding import PartitionSpec as P

DH = 128
TOP = 2


epsilon = 1e-06


def prefix(shard, axis, combine, identity):
    count, index = (lax.axis_size(axis), lax.axis_index(axis))
    everything = lax.all_gather(shard.astype(jnp.bfloat16), axis)
    start = jnp.broadcast_to(jnp.asarray(identity, shard.dtype), shard.shape)

    def turn(k, before):
        reached = k < index
        new = combine(before, everything[k].astype(shard.dtype))
        return jnp.where(reached, new, before)

    return lax.fori_loop(0, count, turn, start)


def add_states(earlier, later):
    return earlier + later


def per_device(
    queries,
    keys,
    values,
    prefix_state,
    out_gain,
    out_weight,
    resid,
    ffn_gain,
    expert_ids,
    route_weights,
    gate_weight,
    up_weight,
    down_weight,
):
    tok_rows = queries.shape[0]
    local_heads = queries.shape[1] // DH
    q_heads = queries.reshape(tok_rows, local_heads, DH)
    k_heads = keys.reshape(tok_rows, local_heads, DH)
    v_heads = values.reshape(tok_rows, local_heads, DH)
    span_state = jnp.einsum("thd,the->hde", k_heads, v_heads, preferred_element_type=jnp.float32)
    earlier = prefix(span_state, "ctx", add_states, jnp.zeros_like(span_state))
    carried = (prefix_state + earlier).astype(jnp.bfloat16)
    scores = jnp.einsum("thd,shd->hts", q_heads, k_heads, preferred_element_type=jnp.float32)
    causal = jnp.arange(tok_rows)[:, None] >= jnp.arange(tok_rows)[None, :]
    scores = jnp.where(causal[None], scores, 0.0).astype(jnp.bfloat16)
    intra = jnp.einsum("hts,shd->thd", scores, v_heads, preferred_element_type=jnp.float32)
    inter = jnp.einsum("thd,hde->the", q_heads, carried, preferred_element_type=jnp.float32)
    raw = intra + inter
    norm_scale = lax.rsqrt(jnp.mean(raw * raw, axis=2, keepdims=True) + epsilon)
    attn = raw * norm_scale * out_gain.astype(jnp.float32).reshape(local_heads, DH)
    attn = attn.astype(jnp.bfloat16).reshape(tok_rows, local_heads * DH)
    partial_out = jnp.dot(
        attn,
        lax.all_gather(out_weight, "ctx", axis=1, tiled=True),
        preferred_element_type=jnp.float32,
    )
    projected = lax.psum_scatter(
        partial_out.astype(jnp.bfloat16), "mdl", scatter_dimension=1, tiled=True
    ).astype(jnp.float32)
    hidden_one = (resid.astype(jnp.float32) + projected).astype(jnp.bfloat16)
    local_experts = gate_weight.shape[0]
    expert_count = lax.axis_size("mdl") * local_experts
    capacity = 3 * tok_rows * TOP // (2 * expert_count)
    owner = lax.axis_index("mdl")
    chosen = expert_ids[:, :, None] == jnp.arange(expert_count, dtype=jnp.int32)[None, None, :]
    uses_count = jnp.sum(chosen.astype(jnp.int32), axis=1)
    slot_index = jnp.cumsum(uses_count, axis=0) - uses_count
    weight_by_expert = jnp.sum(jnp.where(chosen, route_weights[:, :, None], 0.0), axis=1)
    slot_range = jnp.arange(capacity, dtype=jnp.int32)
    placing = (uses_count[None] == 1) & (slot_index[None] == slot_range[:, None, None])
    owned = jnp.arange(expert_count) == owner
    placing_own = jnp.any(placing & owned[None, None, :], axis=2)
    weight_own = jnp.sum(jnp.where(owned[None, :], weight_by_expert, 0.0), axis=1)
    full_rows = lax.all_gather(hidden_one, "mdl", axis=1, tiled=True)
    full_float = full_rows.astype(jnp.float32)
    row_scale = lax.rsqrt(jnp.mean(full_float * full_float, axis=1, keepdims=True) + epsilon)
    normed = (full_float * row_scale * ffn_gain.astype(jnp.float32)).astype(jnp.bfloat16)
    slotted = jnp.dot(
        placing_own.astype(jnp.bfloat16), normed, preferred_element_type=jnp.float32
    ).astype(jnp.bfloat16)
    expert_rows = lax.all_gather(slotted, "ctx", axis=0, tiled=True)
    w_gate = gate_weight[0]
    w_upper = up_weight[0]
    w_down = down_weight[0]
    gate_part = jnp.dot(expert_rows, w_gate, preferred_element_type=jnp.float32)
    up_part = jnp.dot(expert_rows, w_upper, preferred_element_type=jnp.float32)
    inner = (jax.nn.silu(gate_part) * up_part).astype(jnp.bfloat16)
    expert_out = lax.psum_scatter(
        jnp.dot(inner, w_down, preferred_element_type=jnp.float32).astype(jnp.bfloat16),
        "ctx",
        scatter_dimension=0,
        tiled=True,
    ).astype(jnp.float32)
    spread_back = placing_own.astype(jnp.float32).T * weight_own[:, None]
    mixture_part = jnp.dot(spread_back, expert_out, precision=lax.Precision.HIGHEST)
    mixture = lax.psum_scatter(
        mixture_part.astype(jnp.bfloat16), "mdl", scatter_dimension=1, tiled=True
    ).astype(jnp.float32)
    return (hidden_one.astype(jnp.float32) + mixture).astype(jnp.bfloat16)


def solution(mesh):
    placed = (
        P("ctx", "mdl"),
        P("ctx", "mdl"),
        P("ctx", "mdl"),
        P("mdl", None, None),
        P("mdl"),
        P("mdl", "ctx"),
        P("ctx", "mdl"),
        P(),
        P("ctx", None),
        P("ctx", None),
        P("mdl", None, "ctx"),
        P("mdl", None, "ctx"),
        P("mdl", "ctx", None),
    )
    return jax.shard_map(
        per_device, mesh=mesh, in_specs=placed, out_specs=P("ctx", "mdl"), check_vma=False
    )
```

profile of v0, /device:TPU:7, one launch (start us, length us, event | category | flops | bytes accessed | tf_op | source)
XLA Modules:
  0.0 469.5 jit_solution(4389382422263719553)
XLA Ops:
  6.5 0.0 copy-start
  6.5 0.0 all-gather.12.cloned.1.call-start
  6.5 1.2 copy.39
  7.7 0.0 copy-done
  7.7 0.9 convolution_convert_fusion.4
  8.6 0.0 all-gather.12.cloned.1.call-update
  8.7 0.0 all-gather.6.cloned.1.call-start
  8.7 0.7 all-gather.6.cloned.1.call-update
  9.4 0.0 reduce-scatter.4.cloned.1.call-start
  9.5 0.7 bitcast_convert_fusion
  10.2 53.3 %all-gather.12.cloned.1.call-done = bf16[128,128,128]{2,1,0:T(8,128)(2,1)} async-done(((bf16[8,128,128]{2,1,0:T(8,128)(2,1)}), bf16[128,128,128]{2,1,0:T(8,128)(2,1)}) %all-gather.12.cloned.1.call-update) | async-done | bytes 4194320 | tf_op jit(solution)/shard_map/all_gather | solution.py:15
  63.5 20.2 %while.14 = (s32[]{:T(128)}, f32[8,128,128]{2,1,0:T(8,128)S(1)}, s32[]{:T(128)}, bf16[16,8,128,128]{3,2,1,0:T(8,128)(2,1)}, s32[]{:T(128)}, /*index=5*/s32[]{:T(128)}) while((s32[]{:T(128)}, f32[8,128,128]{2,1,0:T(8,128)S(1)}, s32[]{:T(128)}, bf16[16,8,128,128]{3,2,1,0:T(8,128)(2,1)}, s32[]{:T(128)}, /*index=5*/s32[]{:T(128)}) %tuple.50), condition=%wide.region_1.2_spmd.clone, body=%wide.region_0.1_spmd.clone.sunk | while | flops 524292 | bytes 1310813 | solution.py:23
  63.5 1.3 add_select_fusion.2
  64.8 1.2 add_select_fusion.2
  66.1 1.2 add_select_fusion.2
  67.4 1.2 add_select_fusion.2
  68.6 1.2 add_select_fusion.2
  69.9 1.2 add_select_fusion.2
  71.1 1.2 add_select_fusion.2
  72.4 1.2 add_select_fusion.2
  73.6 1.2 add_select_fusion.2
  74.9 1.3 add_select_fusion.2
  76.2 1.2 add_select_fusion.2
  77.5 1.2 add_select_fusion.2
  78.7 1.2 add_select_fusion.2
  80.0 1.2 add_select_fusion.2
  81.2 1.2 add_select_fusion.2
  82.5 1.2 add_select_fusion.2
  83.8 0.3 convolution_bitcast_fusion
  84.1 0.5 multiply_reduce_fusion
  84.6 0.2 multiply_convert_fusion.1
  84.8 79.4 %all-gather.6.cloned.1.call-done = bf16[1024,6144]{1,0:T(8,128)(2,1)} async-done(((bf16[1024,384]{1,0:T(8,128)(2,1)}), bf16[1024,6144]{1,0:T(8,128)(2,1)}) %all-gather.6.cloned.1.call-update) | async-done | bytes 12582928 | tf_op jit(solution)/shard_map/all_gather | solution.py:64
  164.2 7.7 %convolution_convert_fusion.1 = bf16[128,6144]{1,0:T(8,128)(2,1)} fusion(bf16[128,1024]{0,1:T(8,128)(2,1)S(1)} %bitcast.69, bf16[1024,6144]{1,0:T(8,128)(2,1)} %all-gather.6.cloned.1.call-done), kind=kOutput, calls=%fused_computation.2 | convolution fusion | flops 1611399168 | bytes 14417920 | tf_op jit(solution)/shard_map/dot_general | solution.py:62
  171.9 0.0 reduce-scatter.4.cloned.1.call-update
  171.9 0.0 all-gather.8.cloned.1.call-start
  171.9 31.1 %reduce-scatter.4.cloned.1.call-done = bf16[128,768]{1,0:T(8,128)(2,1)} async-done(((bf16[128,6144]{1,0:T(8,128)(2,1)}), bf16[128,768]{1,0:T(8,128)(2,1)}) %reduce-scatter.4.cloned.1.call-update) | async-done | bytes 196624 | tf_op jit(solution)/shard_map/reduce_scatter | solution.py:67
  203.0 1.6 add_convert_fusion.2
  204.7 0.0 all-gather.8.cloned.1.call-update
  204.7 0.0 all-gather.10.cloned.1.call-start
  204.8 0.1 copy.35
  204.9 0.2 reduce_window_sum.11
  205.2 0.1 fusion.29
  205.3 23.4 %all-gather.8.cloned.1.call-done = bf16[128,6144]{1,0:T(8,128)(2,1)} async-done(((bf16[128,768]{1,0:T(8,128)(2,1)}), bf16[128,6144]{1,0:T(8,128)(2,1)}) %all-gather.8.cloned.1.call-update) | async-done | bytes 1572880 | tf_op jit(solution)/shard_map/all_gather | solution.py:84
  228.7 1.8 fusion.5
  230.5 2.9 convolution_convert_fusion.3
  233.4 0.0 all-gather.10.cloned.1.call-update
  233.5 0.0 reduce-scatter.6.cloned.1.call-start
  233.5 77.3 %all-gather.10.cloned.1.call-done = bf16[768,6144]{1,0:T(8,128)(2,1)} async-done(((bf16[48,6144]{1,0:T(8,128)(2,1)}), bf16[768,6144]{1,0:T(8,128)(2,1)}) %all-gather.10.cloned.1.call-update) | async-done | bytes 9437200 | tf_op jit(solution)/shard_map/all_gather | solution.py:91
  310.8 11.0 %fusion.1 = f32[768,576]{0,1:T(8,128)S(1)} fusion(bf16[768,6144]{1,0:T(8,128)(2,1)} %all-gather.10.cloned.1.call-done, bf16[1,6144,576]{1,2,0:T(8,128)(2,1)} %param.26), kind=kOutput, calls=%fused_computation.5 | convolution fusion | flops 5435817984 | bytes 18284544 | tf_op jit(solution)/shard_map/dot_general | solution.py:96
  321.8 0.0 copy-done.9
  321.8 0.0 slice-start.1
  321.8 8.4 %multiply_convert_fusion = bf16[768,576]{0,1:T(8,128)(2,1)S(1)} fusion(f32[768,576]{0,1:T(8,128)S(1)} %fusion.1, bf16[768,6144]{1,0:T(8,128)(2,1)S(1)} %copy-done.9, bf16[1,6144,576]{1,2,0:T(8,128)(2,1)} %param.25), kind=kOutput, calls=%fused_computation.15 | convolution fusion | flops 5438472192 | bytes 19169280 | tf_op jit(solution)/shard_map/dot_general | solution.py:95
  330.2 9.7 %convolution_convert_fusion = bf16[768,6144]{1,0:T(8,128)(2,1)} fusion(bf16[768,576]{0,1:T(8,128)(2,1)S(1)} %multiply_convert_fusion, bf16[1,576,6144]{2,1,0:T(8,128)(2,1)S(1)} %bitcast.72), kind=kOutput, calls=%fused_computation.1 | convolution fusion | flops 5440536576 | bytes 17399808 | tf_op jit(solution)/shard_map/dot_general | solution.py:99
  339.9 0.0 reduce-scatter.6.cloned.1.call-update
  339.9 0.0 copy-start.2
  339.9 0.0 copy-start.1
  339.9 0.0 reduce-scatter.8.cloned.1.call-start
  340.0 0.6 copy-done.8
  340.6 0.1 select_reduce_fusion.1
  340.7 85.7 %reduce-scatter.6.cloned.1.call-done = bf16[48,6144]{1,0:T(8,128)(2,1)} async-done(((bf16[768,6144]{1,0:T(8,128)(2,1)}), bf16[48,6144]{1,0:T(8,128)(2,1)}) %reduce-scatter.6.cloned.1.call-update) | async-done | bytes 589840 | tf_op jit(solution)/shard_map/reduce_scatter | solution.py:98
  426.4 3.6 convolution_convert_fusion.2
  430.0 0.0 reduce-scatter.8.cloned.1.call-update
  430.0 31.0 %reduce-scatter.8.cloned.1.call-done = bf16[128,768]{1,0:T(8,128)(2,1)} async-done(((bf16[128,6144]{1,0:T(8,128)(2,1)}), bf16[128,768]{1,0:T(8,128)(2,1)}) %reduce-scatter.8.cloned.1.call-update) | async-done | bytes 196624 | tf_op jit(solution)/shard_map/reduce_scatter | solution.py:106
  461.0 1.6 add_convert_fusion.1
  (29 shorter events, 0.2 us)
Async XLA Ops:
  6.5 1.2 copy-start
  6.5 57.0 %all-gather.12.cloned.1.call-start = ((), (), s32[]{:S(2)}) async-start(), calls=%async_computation.9 | async-start | bytes 4456448 | tf_op jit(solution)/shard_map/all_gather | solution.py:15
  8.7 155.5 %all-gather.6.cloned.1.call-start = ((), (), s32[]{:S(2)}) async-start(), calls=%async_computation.3 | async-start | bytes 13369344 | tf_op jit(solution)/shard_map/all_gather | solution.py:64
  9.4 193.6 %reduce-scatter.4.cloned.1.call-start = ((), (), s32[]{:S(2)}) async-start(), calls=%async_computation.4 | async-start | bytes 1769472 | tf_op jit(solution)/shard_map/reduce_scatter | solution.py:67
  63.5 20.2 %copy-start.3 = (bf16[128,1024]{1,0:T(8,128)(2,1)S(1)}, bf16[128,1024]{1,0:T(8,128)(2,1)}, u32[]{:S(2)}) copy-start(bf16[128,1024]{1,0:T(8,128)(2,1)} %param.15) | copy-start | bytes 786436
  63.5 20.2 %copy-start.4 = (f32[8,128,128]{2,1,0:T(8,128)S(1)}, f32[8,128,128]{2,1,0:T(8,128)}, u32[]{:S(2)}) copy-start(f32[8,128,128]{2,1,0:T(8,128)} %param.18) | copy-start | bytes 1572868
  164.2 38.8 %copy-start.5 = (bf16[128,768]{1,0:T(8,128)(2,1)S(1)}, bf16[128,768]{1,0:T(8,128)(2,1)}, u32[]{:S(2)}) copy-start(bf16[128,768]{1,0:T(8,128)(2,1)} %param.21) | copy-start | bytes 589828
  164.2 40.6 %copy-start.7 = (s32[128,2]{0,1:T(2,128)S(1)}, s32[128,2]{0,1:T(2,128)}, u32[]{:S(2)}) copy-start(s32[128,2]{0,1:T(2,128)} %param.23) | copy-start | bytes 3076
  164.2 40.9 %copy-start.6 = (bf16[6144]{0:T(1024)(128)(2,1)S(1)}, bf16[6144]{0:T(1024)(128)(2,1)}, u32[]{:S(2)}) copy-start(bf16[6144]{0:T(1024)(128)(2,1)} %param.22) | copy-start | bytes 36868
  171.9 56.8 %all-gather.8.cloned.1.call-start = ((), (), s32[]{:S(2)}) async-start(), calls=%async_computation.5 | async-start | bytes 1769472 | tf_op jit(solution)/shard_map/all_gather | solution.py:84
  204.7 106.0 %all-gather.10.cloned.1.call-start = ((), (), s32[]{:S(2)}) async-start(), calls=%async_computation.6 | async-start | bytes 10027008 | tf_op jit(solution)/shard_map/all_gather | solution.py:91
  233.5 192.9 %reduce-scatter.6.cloned.1.call-start = ((), (), s32[]{:S(2)}) async-start(), calls=%async_computation.7 | async-start | bytes 10027008 | tf_op jit(solution)/shard_map/reduce_scatter | solution.py:98
  310.8 11.0 %copy-start.9 = (bf16[768,6144]{1,0:T(8,128)(2,1)S(1)}, bf16[768,6144]{1,0:T(8,128)(2,1)}, u32[]{:S(2)}) copy-start(bf16[768,6144]{1,0:T(8,128)(2,1)} %all-gather.10.cloned.1.call-done) | copy-start | bytes 28311556
  310.8 19.4 %slice-start = ((s8[7077888]{0:T(1024)(128)(4,1)}), s8[4194304]{0:T(1024)(128)(4,1)S(1)}, s32[]{:S(2)}) async-start(s8[7077888]{0:T(1024)(128)(4,1)} %bitcast.71), calls=%async_computation.10 | async-start | bytes 8388608
  321.8 8.4 %slice-start.1 = ((s8[7077888]{0:T(1024)(128)(4,1)}), s8[2883584]{0:T(1024)(128)(4,1)S(1)}, s32[]{:S(2)}) async-start(s8[7077888]{0:T(1024)(128)(4,1)} %bitcast.71), calls=%async_computation.11 | async-start | bytes 5767168
  339.9 0.7 copy-start.8
  339.9 121.1 %copy-start.2 = (bf16[128,768]{1,0:T(8,128)(2,1)S(1)}, bf16[128,768]{1,0:T(8,128)(2,1)}, u32[]{:S(2)}) copy-start(bf16[128,768]{1,0:T(8,128)(2,1)} %add_convert_fusion.2) | copy-start | bytes 589828
  339.9 122.8 %copy-start.1 = (bf16[128,1024]{1,0:T(8,128)(2,1)S(1)}, bf16[128,1024]{1,0:T(8,128)(2,1)}, u32[]{:S(2)}) copy-start(bf16[128,1024]{1,0:T(8,128)(2,1)} %param.17) | copy-start | bytes 786436
  339.9 121.1 %reduce-scatter.8.cloned.1.call-start = ((), (), s32[]{:S(2)}) async-start(), calls=%async_computation.8 | async-start | bytes 1769472 | tf_op jit(solution)/shard_map/reduce_scatter | solution.py:106
Sparse Core Ops, SparseCore 0:
  9.5 53.9 all-gather.11
  65.6 98.5 all-gather.5
  172.0 30.9 reduce-scatter.3
  204.8 23.8 all-gather.7
  233.6 77.1 all-gather.9
  340.0 86.2 reduce-scatter.5
  430.2 30.8 reduce-scatter.7
where the time goes:
time: 472 us; the launch traced here: 470 us
  waiting for transfers between devices  382 us (81%)
  matrix products  45 us (10%)
  other arithmetic  26.3 us (6%)
  between operations  13.7 us (3%)
    reduce_scatter x1, waiting for transfers between devices, per_device(): lax.psum_scatter(jnp.dot(inner, w_down, preferred_element_type=jnp.float3...  85.7 us
    all_gather x1, waiting for transfers between devices, per_device(): lax.all_gather(out_weight, 'ctx', axis=1, tiled=True)  79.4 us
    all_gather x1, waiting for transfers between devices, per_device(): expert_rows = lax.all_gather(slotted, 'ctx', axis=0, tiled=True)  77.3 us
    all_gather x1, waiting for transfers between devices, prefix(): everything = lax.all_gather(shard.astype(jnp.bfloat16), axis)  53.3 us
    reduce_scatter x1, waiting for transfers between devices, per_device(): lax.psum_scatter(partial_out.astype(jnp.bfloat16), 'mdl', scatter_dimensi...  31.1 us
    reduce_scatter x1, waiting for transfers between devices, per_device(): lax.psum_scatter(mixture_part.astype(jnp.bfloat16), 'mdl', scatter_dimens...  31 us
    all_gather x1, waiting for transfers between devices, per_device(): full_rows = lax.all_gather(hidden_one, 'mdl', axis=1, tiled=True)  23.4 us
    select_n x16, other arithmetic, turn(): return jnp.where(reached, new, before)  19.9 us
  transfers between devices with their start and end apart: 7, of which 7 were waited for; matrix products, arithmetic and copies ran while one was open for 5% of the time, Pallas kernels for 0%

commit v1 on v0

v1 whole, which is shorter than its diff:
```python
import jax
import jax.numpy as jnp
from jax import lax
from jax.sharding import PartitionSpec as P

DH = 128
TOP = 2
N = 4

epsilon = 1e-06
f32 = jnp.float32
bf16 = jnp.bfloat16


def move_z(v, s):
    return lax.ppermute(v, "ctx", [(y * N + z, y * N + (z + s) % N) for y in range(N) for z in range(N)])


def move_y(v, s):
    return lax.ppermute(v, "ctx", [(y * N + z, (y + s) % N * N + z) for y in range(N) for z in range(N)])


def move_m(v, s, flip):
    return lax.ppermute(v, "mdl", [(x * 2 + c, (x + s) % N * 2 + (c ^ flip)) for x in range(N) for c in range(2)])


def swap_xy(v):
    pairs = []
    for y in range(N):
        for z in range(N):
            for x in range(N):
                for c in range(2):
                    pairs.append(((y * N + z) * 8 + x * 2 + c, (x * N + z) * 8 + y * 2 + c))
    return lax.ppermute(v, ("ctx", "mdl"), pairs)


def in_order(parts, at, axis):
    turned = [parts[3], parts[2], parts[1], parts[0]]
    size = parts[0].shape[axis]
    both = jnp.concatenate(turned + turned[:3], axis=axis)
    return lax.dynamic_slice_in_dim(both, (3 - at) * size, 4 * size, axis=axis)


def ring_gather(v, move):
    half = v.shape[0] // 2
    back, ahead = move(v, 1), move(v, -1)
    far = jnp.concatenate([move(back[:half], 1), move(ahead[half:], -1)], axis=0)
    return [v, back, far, ahead]


def ring_scatter(parts, move):
    half = parts[2].shape[0] // 2
    wide = parts[2].astype(bf16)
    a = move(wide[:half], 1)
    b = move(wide[half:], -1)
    p1, p3 = parts[1].astype(f32), parts[3].astype(f32)
    ahead = jnp.concatenate([p1[:half] + a.astype(f32), p1[half:]], axis=0).astype(bf16)
    behind = jnp.concatenate([p3[:half], p3[half:] + b.astype(f32)], axis=0).astype(bf16)
    return parts[0].astype(f32) + move(ahead, 1).astype(f32) + move(behind, -1).astype(f32)


def carried_state(span, prefix_state, y, z):
    quarter = span.shape[0] // N
    span = span.astype(bf16)

    def cut(a, q):
        return lax.dynamic_slice_in_dim(a, q % N * quarter, quarter, axis=0)

    mine = [cut(span, z).astype(f32)]
    for s in (1, 2, 3):
        mine.append(move_z(cut(span, z + s), s).astype(f32))
    total = (mine[0] + mine[1] + mine[2] + mine[3]).astype(bf16)
    base = cut(prefix_state, z)
    for s in (1, 2, 3):
        base = base + jnp.where((y - s) % N < y, move_y(total, s).astype(f32), 0.0)
    out = []
    for r in range(N):
        target = (z + r) % N
        acc = base
        for s in range(N):
            acc = acc + jnp.where((z - s) % N < target, mine[s], 0.0)
        acc = acc.astype(bf16)
        out.append(acc if r == 0 else move_z(acc, r))
    return in_order(out, z, 0)


def attention(queries, keys, values, prefix_state, out_gain, y, z):
    rows = queries.shape[0]
    heads = queries.shape[1] // DH
    q = queries.reshape(rows, heads, DH)
    k = keys.reshape(rows, heads, DH)
    v = values.reshape(rows, heads, DH)
    span = jnp.einsum("thd,the->hde", k, v, preferred_element_type=f32)
    carried = carried_state(span, prefix_state, y, z)
    scores = jnp.einsum("thd,shd->hts", q, k, preferred_element_type=f32)
    causal = jnp.arange(rows)[:, None] >= jnp.arange(rows)[None, :]
    scores = jnp.where(causal[None], scores, 0.0).astype(bf16)
    intra = jnp.einsum("hts,shd->thd", scores, v, preferred_element_type=f32)
    inter = jnp.einsum("thd,hde->the", q, carried, preferred_element_type=f32)
    raw = intra + inter
    scale = lax.rsqrt(jnp.mean(raw * raw, axis=2, keepdims=True) + epsilon)
    attn = raw * scale * out_gain.astype(f32).reshape(heads, DH)
    return attn.astype(bf16).reshape(rows, heads * DH)


def per_device(
    queries,
    keys,
    values,
    prefix_state,
    out_gain,
    out_weight,
    resid,
    ffn_gain,
    expert_ids,
    route_weights,
    gate_weight,
    up_weight,
    down_weight,
):
    ctx, mdl = lax.axis_index("ctx"), lax.axis_index("mdl")
    y, z = ctx // N, ctx % N
    x, c = mdl // 2, mdl % 2
    rows = queries.shape[0]
    cols = resid.shape[1]
    experts = 2 * N
    cap = 3 * rows * TOP // (2 * experts)
    places = [(s, flip) for s in range(N) for flip in range(2)]

    own_resid = swap_xy(resid)
    routing = jnp.concatenate([expert_ids.astype(f32), route_weights], axis=1)
    routing = lax.all_gather(routing, "ctx")[x * N + z]
    ids, weights = routing[:, :TOP].astype(jnp.int32), routing[:, TOP:]
    chosen = ids[:, :, None] == jnp.arange(experts, dtype=jnp.int32)
    uses = jnp.sum(chosen.astype(jnp.int32), axis=1)
    slots = jnp.cumsum(uses, axis=0) - uses
    slot_of = jnp.sum(jnp.where(chosen, slots[:, None, :], 0), axis=2)

    w_parts = ring_gather(out_weight, move_z)
    w_full = in_order(w_parts, z, 1)
    attn = attention(queries, keys, values, prefix_state, out_gain, y, z)
    a_full = in_order(ring_gather(attn, move_y), y, 0)
    partial = jnp.dot(a_full, w_full, preferred_element_type=f32).astype(bf16)
    partial = partial.reshape(N, rows, 2, cols)
    kept = lax.dynamic_index_in_dim(partial, c, axis=2, keepdims=False)
    given = lax.dynamic_index_in_dim(partial, 1 - c, axis=2, keepdims=False)
    pair = (kept.astype(f32) + move_m(given, 0, 1).astype(f32)).astype(bf16)
    summed = own_resid.astype(f32) + lax.dynamic_index_in_dim(pair, x, 0, keepdims=False).astype(f32)
    for s in (1, 2, 3):
        piece = lax.dynamic_index_in_dim(pair, (x + s) % N, 0, keepdims=False)
        summed = summed + move_m(piece, s, 0).astype(f32)
    hidden_one = summed.astype(bf16)

    slot_range = jnp.arange(cap, dtype=jnp.int32)
    dispatched = [[None, None] for _ in range(N)]
    for s, flip in places:
        expert = (x + s) % N * 2 + (c ^ flip)
        placing = jnp.any((ids[None] == expert) & (slot_of[None] == slot_range[:, None, None]), axis=2)
        picked = jnp.dot(placing.astype(bf16), hidden_one, preferred_element_type=f32).astype(bf16)
        dispatched[s][flip] = picked if (s, flip) == (0, 0) else move_m(picked, s, flip)
    tiles = []
    gain = lax.dynamic_slice_in_dim(ffn_gain, y * 2 * cols, 2 * cols, 0).astype(f32)
    squares = []
    for s in range(N):
        same, other = dispatched[s]
        tile = jnp.concatenate([jnp.where(c == 0, same, other), jnp.where(c == 0, other, same)], axis=1).astype(f32)
        squares.append(jnp.sum(tile * tile, axis=1))
        tiles.append((tile * gain).astype(bf16))
    squares = lax.all_gather(jnp.stack(squares), "ctx").reshape(N, N, N, cap)
    squares = jnp.sum(squares, axis=0)
    row_scale = lax.rsqrt(squares / (2 * N * cols) + epsilon)

    w_gate, w_up, w_down = gate_weight[0], up_weight[0], down_weight[0]

    def gather(first, second):
        over_z = ring_gather(first, move_z)
        over_y = ring_gather(second, move_y)
        one = ring_gather(jnp.concatenate(over_z, axis=0), move_y)
        two = ring_gather(jnp.concatenate([over_y[k] for k in range(N)], axis=0), move_z)
        full = []
        for k in range(N):
            here = [one[k]]
            for j in range(N):
                here.append(two[j][k * cap : (k + 1) * cap])
            full.append(jnp.concatenate(here, axis=0))
        return in_order(full, y, 1)

    def scale_rows(i):
        order = [lax.dynamic_index_in_dim(row_scale, (z - k) % N, 0, keepdims=False)[i] for k in range(N)]
        return jnp.concatenate(order)

    def experts_on(xs, i):
        scale = jnp.concatenate([scale_rows(i), scale_rows(i + 1)])[:, None]
        gate = jnp.dot(xs, w_gate, preferred_element_type=f32) * scale
        up = jnp.dot(xs, w_up, preferred_element_type=f32) * scale
        inner = (jax.nn.silu(gate) * up).astype(bf16)
        return jnp.dot(inner, w_down, preferred_element_type=f32).astype(bf16)

    def scatter(out):
        one, two = out[: N * cap], out[N * cap :]
        width = 2 * cols
        by_y = [lax.dynamic_slice_in_dim(one, (y + r) % N * width, width, axis=1) for r in range(N)]
        one = ring_scatter(by_y, move_y)
        one = one.reshape(N, cap, width)
        one = ring_scatter([one[(N - r) % N] for r in range(N)], move_z)
        two = two.reshape(N, cap, N * width)
        two = ring_scatter([two[(N - r) % N] for r in range(N)], move_z)
        by_y = [lax.dynamic_slice_in_dim(two, (y + r) % N * width, width, axis=1) for r in range(N)]
        two = ring_scatter(by_y, move_y)
        return one, two

    xs = [gather(tiles[i], tiles[i + 1]) for i in (0, 2)]
    outs = [experts_on(xs[i // 2], i) for i in (0, 2)]
    back = []
    for o in outs:
        back += scatter(o)

    mixture = 0.0
    for s, flip in places:
        piece = back[(N - s) % N].astype(bf16)
        piece = lax.dynamic_slice_in_dim(piece, (c ^ flip) * cols, cols, axis=1)
        piece = piece if (s, flip) == (0, 0) else move_m(piece, s, flip)
        expert = (x - s) % N * 2 + (c ^ flip)
        for j in range(TOP):
            taken = (ids[:, j : j + 1] == expert) & (slot_of[:, j : j + 1] == slot_range[None, :])
            mixture = mixture + weights[:, j : j + 1] * jnp.dot(taken.astype(bf16), piece, preferred_element_type=f32)
    layer_out = (hidden_one.astype(f32) + mixture).astype(bf16)
    return swap_xy(layer_out)


def solution(mesh):
    placed = (
        P("ctx", "mdl"),
        P("ctx", "mdl"),
        P("ctx", "mdl"),
        P("mdl", None, None),
        P("mdl"),
        P("mdl", "ctx"),
        P("ctx", "mdl"),
        P(),
        P("ctx", None),
        P("ctx", None),
        P("mdl", None, "ctx"),
        P("mdl", None, "ctx"),
        P("mdl", "ctx", None),
    )
    return jax.shard_map(
        per_device, mesh=mesh, in_specs=placed, out_specs=P("ctx", "mdl"), check_vma=False
    )
```

time: 472 us -> 438 us (0.928); the launches traced: 470 us -> 430 us
  waiting for transfers between devices: 382 us -> 86.8 us
  starting transfers between devices: 0.25 us -> 150 us
  local copies, waits for them, and re-layouts: 1.94 us -> 83.8 us
  blocking collectives: 0 us -> 43.7 us
  other arithmetic: 26.3 us -> 11.1 us
  between operations: 13.7 us -> 2.9 us
  matrix products: 45 us -> 51.6 us
    all_gather x4 -> x0, waiting for transfers between devices: 233 us -> none  [the longest x1 79.4 us: per_device(): lax.all_gather(out_weight, 'ctx', axis=1, tiled=True)]
    ppermute x0 -> x101, starting transfers between devices: none -> 150 us  [the longest x18 50.8 us: move_m(): lax.ppermute(v, 'mdl', [(x * 2 + c, (x + s) % N * 2 + (c ^ flip)) for x i...]
    reduce_scatter x3 -> x0, waiting for transfers between devices: 148 us -> none  [the longest x1 85.7 us: per_device(): lax.psum_scatter(jnp.dot(inner, w_down, preferred_element_type=jnp.float3...]
    ppermute x0 -> x101, waiting for transfers between devices: none -> 86.8 us  [the longest x42 32.1 us: move_z(): lax.ppermute(v, 'ctx', [(y * N + z, y * N + (z + s) % N) for y in range(N...]
    unnamed x24 -> x228, local copies, waits for them, and re-layouts: 0.63 us -> 60.8 us
    all_gather x0 -> x2, blocking collectives: none -> 43.7 us  [the longest x1 26 us: per_device(): routing = lax.all_gather(routing, 'ctx')[x * N + z]]
    select_n x16 -> x3, other arithmetic: 19.9 us -> 0.04 us  [per_device(): jnp.where(c == 0, same, other)]
    concatenate x0 -> x11, local copies, waits for them, and re-layouts: none -> 9.07 us  [the longest x5 5.44 us: in_order(): both = jnp.concatenate(turned + turned[:3], axis=axis)]
  transfers between devices with their start and end apart: 7 -> 101, of which waited for: 7 -> 33; matrix products, arithmetic and copies ran while one was open for 5% -> 29% of each run, Pallas kernels for 0% -> 0%
where the time goes in v1:
time: 438 us; the launch traced here: 430 us
  starting transfers between devices  150 us (34%)
  waiting for transfers between devices  86.8 us (20%)
  local copies, waits for them, and re-layouts  83.8 us (19%)
  matrix products  51.6 us (12%)
  blocking collectives  43.7 us (10%)
  other arithmetic  11.1 us (3%)
    unnamed x228, local copies, waits for them, and re-layouts  60.8 us
    ppermute x18, starting transfers between devices, move_m(): lax.ppermute(v, 'mdl', [(x * 2 + c, (x + s) % N * 2 + (c ^ flip)) for x i...  50.8 us
    ppermute x42, starting transfers between devices, move_z(): lax.ppermute(v, 'ctx', [(y * N + z, y * N + (z + s) % N) for y in range(N...  50.5 us
    ppermute x39, starting transfers between devices, move_y(): lax.ppermute(v, 'ctx', [(y * N + z, (y + s) % N * N + z) for y in range(N...  43.2 us
    ppermute x42, waiting for transfers between devices, move_z(): lax.ppermute(v, 'ctx', [(y * N + z, y * N + (z + s) % N) for y in range(N...  32.1 us
    all_gather x1, blocking collectives, per_device(): routing = lax.all_gather(routing, 'ctx')[x * N + z]  26 us
    ppermute x39, waiting for transfers between devices, move_y(): lax.ppermute(v, 'ctx', [(y * N + z, (y + s) % N * N + z) for y in range(N...  23.4 us
    ppermute x18, waiting for transfers between devices, move_m(): lax.ppermute(v, 'mdl', [(x * 2 + c, (x + s) % N * 2 + (c ^ flip)) for x i...  17.7 us
  transfers between devices with their start and end apart: 101, of which 33 were waited for; matrix products, arithmetic and copies ran while one was open for 29% of the time, Pallas kernels for 0%

profile of v1, /device:TPU:7, one launch (start us, length us, event | category | flops | bytes accessed | tf_op | source)
XLA Modules:
  0.0 430.0 jit_solution(9349084748699111921)
XLA Ops:
  0.0 3.8 collective-permute-start.14
  6.1 2.7 collective-permute-start.3
  13.1 26.0 %all-gather = f32[2048,4]{0,1:T(4,128)S(1)} all-gather(f32[128,4]{0,1:T(4,128)S(1)} %pad_maximum_fusion.21), channel_id=2, replica_groups=mesh['ctx'=16,'mdl'=8] {'ctx'}, dimensions={0}, use_global_device_ids=true | all-gather | bytes 34816 | tf_op jit(solution)/shard_map/all_gather | solution.py:132
  42.3 3.5 collective-permute-start
  47.0 2.3 collective-permute-start.7
  49.3 1.6 collective-permute-start.8
  54.0 2.1 collective-permute-done.9
  63.0 2.2 collective-permute-done.11
  66.0 2.9 collective-permute-start.13
  69.2 3.8 collective-permute-done.12
  73.0 1.7 collective-permute-done.13
  74.7 3.7 concatenate.150
  80.8 1.9 fusion.16
  83.0 3.2 constant_dynamic-slice_fusion.17
  86.4 9.9 %collective-permute-start.18 = (bf16[4,128,768]{2,1,0:T(8,128)(2,1)S(1)}, bf16[4,128,768]{2,1,0:T(8,128)(2,1)S(1)}, u32[]{:S(2)}, u32[]{:S(2)}) collective-permute-start(bf16[4,128,768]{2,1,0:T(8,128)(2,1)S(1)} %bitcast.204), channel_id=1, source_target_pairs={{0,1},{1,0},{2,3},{3,2},{4,5},{5,4},{6,7},{7,6},{8,9},{9,8},{10,11... | collective-permute-start | bytes 2359304 | tf_op jit(solution)/shard_map/ppermute | solution.py:24
  102.1 3.5 collective-permute-done.19
  105.6 5.8 %collective-permute-done.21 = bf16[128,768]{1,0:T(8,128)(2,1)S(1)} collective-permute-done((bf16[128,768]{1,0:T(8,128)(2,1)S(1)}, bf16[128,768]{1,0:T(8,128)(2,1)S(1)}, u32[]{:S(2)}, u32[]{:S(2)}) %collective-permute-start.21) | collective-permute-done | bytes 196640 | tf_op jit(solution)/shard_map/ppermute | solution.py:24
  116.5 1.9 collective-permute-start.41
  121.9 2.6 collective-permute-done.42
  124.5 1.6 collective-permute-done.43
  128.7 3.1 collective-permute-start.59
  131.7 2.7 collective-permute-start.30
  135.0 17.7 %all-gather.2 = f32[16,4,48]{2,1,0:T(4,128)S(1)} all-gather(f32[1,4,48]{2,1,0:T(4,128)S(1)} %maximum_bitcast_fusion), channel_id=3, replica_groups=mesh['ctx'=16,'mdl'=8] {'ctx'}, dimensions={0}, use_global_device_ids=true | all-gather | bytes 13056 | tf_op jit(solution)/shard_map/all_gather | solution.py:169
  155.6 1.9 collective-permute-start.25
  160.9 1.7 collective-permute-start.62
  162.7 2.7 collective-permute-start.33
  165.5 2.7 collective-permute-start.26
  171.0 3.4 collective-permute-done.55
  174.4 1.8 collective-permute-start.57
  177.8 2.6 collective-permute-start.27
  185.2 8.7 %collective-permute-done.58 = bf16[192,1536]{1,0:T(8,128)(2,1)S(1)} collective-permute-done((bf16[192,1536]{1,0:T(8,128)(2,1)}, bf16[192,1536]{1,0:T(8,128)(2,1)S(1)}, u32[]{:S(2)}, u32[]{:S(2)}) %collective-permute-start.58) | collective-permute-done | bytes 589856 | tf_op jit(solution)/shard_map/ppermute | solution.py:20
  195.5 3.0 collective-permute-start.64
  200.2 2.7 collective-permute-start.35
  206.8 2.1 collective-permute-start.39
  212.0 3.0 collective-permute-start.68
  216.6 3.0 collective-permute-start.65
  220.6 1.6 slice_dynamic-update-slice_fusion.40
  222.2 4.3 collective-permute-done.65
  228.9 3.4 collective-permute-start.36
  252.6 1.6 slice_dynamic-update-slice_fusion
  271.8 7.6 %fusion.35 = f32[384,576]{0,1:T(8,128)S(1)} fusion(bf16[1,6144,576]{1,2,0:T(8,128)(2,1)} %param.24, bf16[384,10752]{1,0:T(8,128)(2,1)} %slice_dynamic-update-slice_fusion.7, s32[]{:T(128)S(6)} %select_n.563, f32[384]{0:T(512)S(1)} %concatenate.177), kind=kOutput, calls=%fused_computation.24 | convolution fusion | flops 2718130176 | bytes 12682756 | tf_op jit(solution)/shard_map/dot_general | solution.py:195
  279.4 6.2 %fusion.25 = f32[384,576]{0,1:T(8,128)S(1)} fusion(bf16[1,6144,576]{1,2,0:T(8,128)(2,1)} %param.23, bf16[384,10752]{1,0:T(8,128)(2,1)S(1)} %copy-done.37, s32[]{:T(128)S(6)} %select_n.563, f32[384]{0:T(512)S(1)} %concatenate.177), kind=kOutput, calls=%fused_computation.22 | convolution fusion | flops 2718130176 | bytes 12683268 | tf_op jit(solution)/shard_map/dot_general | solution.py:194
  285.6 7.5 %convolution_convert_fusion = bf16[384,6144]{1,0:T(8,128)(2,1)S(1)} fusion(bf16[1,576,6144]{2,1,0:T(8,128)(2,1)} %param.25, f32[384,576]{0,1:T(8,128)S(1)} %fusion.35, f32[384,576]{0,1:T(8,128)S(1)} %fusion.25), kind=kOutput, calls=%fused_computation | convolution fusion | flops 2721595392 | bytes 13565952 | tf_op jit(solution)/shard_map/dot_general | solution.py:197
  300.3 6.1 %fusion.30 = f32[384,576]{0,1:T(8,128)S(1)} fusion(bf16[1,6144,576]{1,2,0:T(8,128)(2,1)} %param.24, bf16[384,10752]{1,0:T(8,128)(2,1)S(1)} %slice_dynamic-update-slice_fusion.25, s32[]{:T(128)S(6)} %select_n.563, f32[384]{0:T(512)S(1)} %concatenate.165), kind=kOutput, calls=%fused_computation.23 | convolution fusion | flops 2718130176 | bytes 12683268 | tf_op jit(solution)/shard_map/dot_general | solution.py:195
  306.4 6.1 %fusion.20 = f32[384,576]{0,1:T(8,128)S(1)} fusion(bf16[1,6144,576]{1,2,0:T(8,128)(2,1)} %param.23, bf16[384,10752]{1,0:T(8,128)(2,1)S(1)} %slice_dynamic-update-slice_fusion.25, s32[]{:T(128)S(6)} %select_n.563, f32[384]{0:T(512)S(1)} %concatenate.165), kind=kOutput, calls=%fused_computation.21 | convolution fusion | flops 2718130176 | bytes 12683268 | tf_op jit(solution)/shard_map/dot_general | solution.py:194
  313.4 2.1 collective-permute-start.72
  315.5 7.5 %convolution_convert_fusion.1 = bf16[384,6144]{1,0:T(8,128)(2,1)S(1)} fusion(bf16[1,576,6144]{2,1,0:T(8,128)(2,1)} %param.25, f32[384,576]{0,1:T(8,128)S(1)} %fusion.30, f32[384,576]{0,1:T(8,128)S(1)} %fusion.20), kind=kOutput, calls=%fused_computation.1 | convolution fusion | flops 2721595392 | bytes 13565952 | tf_op jit(solution)/shard_map/dot_general | solution.py:197
  323.6 2.7 collective-permute-start.82
  326.3 2.7 collective-permute-start.92
  330.3 1.7 collective-permute-start.47
  338.0 4.8 %collective-permute-done.73 = bf16[48,6144]{1,0:T(8,128)(2,1)S(1)} collective-permute-done((bf16[48,6144]{1,0:T(8,128)(2,1)S(1)}, bf16[48,6144]{1,0:T(8,128)(2,1)S(1)}, u32[]{:S(2)}, u32[]{:S(2)}) %collective-permute-start.73) | collective-permute-done | bytes 589856 | tf_op jit(solution)/shard_map/ppermute | solution.py:16
  342.9 1.7 collective-permute-start.48
  345.0 2.9 collective-permute-done.81
  348.2 3.5 collective-permute-done.93
  351.7 4.5 %collective-permute-done.91 = bf16[48,6144]{1,0:T(8,128)(2,1)S(1)} collective-permute-done((bf16[48,6144]{1,0:T(8,128)(2,1)S(1)}, bf16[48,6144]{1,0:T(8,128)(2,1)S(1)}, u32[]{:S(2)}, u32[]{:S(2)}) %collective-permute-start.91) | collective-permute-done | bytes 589856 | tf_op jit(solution)/shard_map/ppermute | solution.py:16
  356.7 2.7 collective-permute-start.86
  359.9 2.7 collective-permute-start.96
  363.0 2.7 collective-permute-start.51
  373.4 1.6 collective-permute-done.85
  375.4 23.9 %collective-permute-start.79 = (bf16[48,768]{1,0:T(8,128)(2,1)S(1)}, bf16[48,768]{1,0:T(8,128)(2,1)S(1)}, u32[]{:S(2)}, u32[]{:S(2)}) collective-permute-start(bf16[48,768]{1,0:T(8,128)(2,1)S(1)} %get-tuple-element.82), channel_id=1, source_target_pairs={{0,3},{1,2},{2,5},{3,4},{4,7},{5,6},{6,1},{7,0},{8,11},{9,10},{10,... | collective-permute-start | bytes 221192 | tf_op jit(solution)/shard_map/ppermute | solution.py:24
  401.0 3.0 collective-permute-start.89
  408.3 2.5 collective-permute-done.99
  413.1 2.2 collective-permute-start.100
  415.3 13.6 %collective-permute-done.100 = bf16[128,768]{1,0:T(8,128)(2,1)S(1)} collective-permute-done((bf16[128,768]{1,0:T(8,128)(2,1)S(1)}, bf16[128,768]{1,0:T(8,128)(2,1)S(1)}, u32[]{:S(2)}, u32[]{:S(2)}) %collective-permute-start.100) | collective-permute-done | bytes 196640 | tf_op jit(solution)/shard_map/ppermute | solution.py:34
  (531 shorter events, 143.9 us)
Async XLA Ops:
  0.0 59.6 %collective-permute-start.14 = (bf16[1024,384]{1,0:T(8,128)(2,1)}, bf16[1024,384]{1,0:T(8,128)(2,1)S(1)}, u32[]{:S(2)}, u32[]{:S(2)}) collective-permute-start(bf16[1024,384]{1,0:T(8,128)(2,1)} %param.18), channel_id=1, source_target_pairs={{0,24},{8,0},{16,8},{24,16},{32,56},{40,32},{48,40},{56,48},{64,88... | collective-permute-start | bytes 2359304 | tf_op jit(solution)/shard_map/ppermute | solution.py:16
  3.8 58.1 %collective-permute-start.15 = (bf16[1024,384]{1,0:T(8,128)(2,1)}, bf16[1024,384]{1,0:T(8,128)(2,1)S(1)}, u32[]{:S(2)}, u32[]{:S(2)}) collective-permute-start(bf16[1024,384]{1,0:T(8,128)(2,1)} %param.18), channel_id=1, source_target_pairs={{0,8},{8,16},{16,24},{24,0},{32,40},{40,48},{48,56},{56,32},{64,72... | collective-permute-start | bytes 2359304 | tf_op jit(solution)/shard_map/ppermute | solution.py:16
  6.1 33.0 %collective-permute-start.3 = (bf16[2,128,128]{2,1,0:T(8,128)(2,1)S(1)}, bf16[2,128,128]{2,1,0:T(8,128)(2,1)S(1)}, u32[]{:S(2)}, u32[]{:S(2)}) collective-permute-start(bf16[2,128,128]{2,1,0:T(8,128)(2,1)S(1)} %get-tuple-element.78), channel_id=1, source_target_pairs={{0,24},{8,0},{16,8},{24,16},{32,56},{40,32},{48,40},{56,48},{64,88... | collective-permute-start | bytes 196616 | tf_op jit(solution)/shard_map/ppermute | solution.py:16
  8.9 30.2 %collective-permute-start.2 = (bf16[2,128,128]{2,1,0:T(8,128)(2,1)S(1)}, bf16[2,128,128]{2,1,0:T(8,128)(2,1)S(1)}, u32[]{:S(2)}, u32[]{:S(2)}) collective-permute-start(bf16[2,128,128]{2,1,0:T(8,128)(2,1)S(1)} %get-tuple-element.79), channel_id=1, source_target_pairs={{0,16},{8,24},{16,0},{24,8},{32,48},{40,56},{48,32},{56,40},{64,80... | collective-permute-start | bytes 196616 | tf_op jit(solution)/shard_map/ppermute | solution.py:16
  8.9 30.2 %collective-permute-start.1 = (bf16[2,128,128]{2,1,0:T(8,128)(2,1)S(1)}, bf16[2,128,128]{2,1,0:T(8,128)(2,1)S(1)}, u32[]{:S(2)}, u32[]{:S(2)}) collective-permute-start(bf16[2,128,128]{2,1,0:T(8,128)(2,1)S(1)} %get-tuple-element.80), channel_id=1, source_target_pairs={{0,8},{8,16},{16,24},{24,0},{32,40},{40,48},{48,56},{56,32},{64,72... | collective-permute-start | bytes 196616 | tf_op jit(solution)/shard_map/ppermute | solution.py:16
  42.3 59.7 %collective-permute-start = (bf16[128,768]{1,0:T(8,128)(2,1)}, bf16[128,768]{1,0:T(8,128)(2,1)}, u32[]{:S(2)}, u32[]{:S(2)}) collective-permute-start(bf16[128,768]{1,0:T(8,128)(2,1)} %param.19), channel_id=1, source_target_pairs={{0,0},{1,1},{2,32},{3,33},{4,64},{5,65},{6,96},{7,97},{8,8},{9,9},... | collective-permute-start | bytes 589832 | tf_op jit(solution)/shard_map/ppermute | solution.py:34
  56.8 8.4 %collective-permute-start.11 = (bf16[128,1024]{0,1:T(8,128)(2,1)S(1)}, bf16[128,1024]{0,1:T(8,128)(2,1)S(1)}, u32[]{:S(2)}, u32[]{:S(2)}) collective-permute-start(bf16[128,1024]{0,1:T(8,128)(2,1)S(1)} %bitcast.200), channel_id=1, source_target_pairs={{0,32},{8,40},{16,48},{24,56},{32,64},{40,72},{48,80},{56,88},{64,... | collective-permute-start | bytes 786440 | tf_op jit(solution)/shard_map/ppermute | solution.py:20
  60.4 18.1 %collective-permute-start.17 = (bf16[512,384]{1,0:T(8,128)(2,1)}, bf16[512,384]{1,0:T(8,128)(2,1)S(1)}, u32[]{:S(2)}, u32[]{:S(2)}) collective-permute-start(bf16[512,384]{1,0:T(8,128)(2,1)} %slice.666), channel_id=1, source_target_pairs={{0,24},{8,0},{16,8},{24,16},{32,56},{40,32},{48,40},{56,48},{64,88... | collective-permute-start | bytes 1179656 | tf_op jit(solution)/shard_map/ppermute | solution.py:16
  62.6 15.9 %collective-permute-start.16 = (bf16[512,384]{1,0:T(8,128)(2,1)}, bf16[512,384]{1,0:T(8,128)(2,1)S(1)}, u32[]{:S(2)}, u32[]{:S(2)}) collective-permute-start(bf16[512,384]{1,0:T(8,128)(2,1)} %slice.665), channel_id=1, source_target_pairs={{0,8},{8,16},{16,24},{24,0},{32,40},{40,48},{48,56},{56,32},{64,72... | collective-permute-start | bytes 1179656 | tf_op jit(solution)/shard_map/ppermute | solution.py:16
  65.2 7.8 %collective-permute-start.12 = (bf16[64,1024]{0,1:T(8,128)(2,1)S(1)}, bf16[64,1024]{0,1:T(8,128)(2,1)S(1)}, u32[]{:S(2)}, u32[]{:S(2)}) collective-permute-start(bf16[64,1024]{0,1:T(8,128)(2,1)S(1)} %bitcast.203), channel_id=1, source_target_pairs={{0,32},{8,40},{16,48},{24,56},{32,64},{40,72},{48,80},{56,88},{64,... | collective-permute-start | bytes 393224 | tf_op jit(solution)/shard_map/ppermute | solution.py:20
  66.0 8.7 %collective-permute-start.13 = (bf16[64,1024]{0,1:T(8,128)(2,1)}, bf16[64,1024]{0,1:T(8,128)(2,1)}, u32[]{:S(2)}, u32[]{:S(2)}) collective-permute-start(bf16[64,1024]{0,1:T(8,128)(2,1)} %slice.664), channel_id=1, source_target_pairs={{0,96},{8,104},{16,112},{24,120},{32,0},{40,8},{48,16},{56,24},{64... | collective-permute-start | bytes 393224 | tf_op jit(solution)/shard_map/ppermute | solution.py:20
  86.4 12.5 %collective-permute-start.18 = (bf16[4,128,768]{2,1,0:T(8,128)(2,1)S(1)}, bf16[4,128,768]{2,1,0:T(8,128)(2,1)S(1)}, u32[]{:S(2)}, u32[]{:S(2)}) collective-permute-start(bf16[4,128,768]{2,1,0:T(8,128)(2,1)S(1)} %bitcast.204), channel_id=1, source_target_pairs={{0,1},{1,0},{2,3},{3,2},{4,5},{5,4},{6,7},{7,6},{8,9},{9,8},{10,11... | collective-permute-start | bytes 2359304 | tf_op jit(solution)/shard_map/ppermute | solution.py:24
  99.9 11.5 %collective-permute-start.21 = (bf16[128,768]{1,0:T(8,128)(2,1)S(1)}, bf16[128,768]{1,0:T(8,128)(2,1)S(1)}, u32[]{:S(2)}, u32[]{:S(2)}) collective-permute-start(bf16[128,768]{1,0:T(8,128)(2,1)S(1)} %get-tuple-element.66), channel_id=1, source_target_pairs={{0,6},{1,7},{2,0},{3,1},{4,2},{5,3},{6,4},{7,5},{8,14},{9,15},{10,... | collective-permute-start | bytes 589832 | tf_op jit(solution)/shard_map/ppermute | solution.py:24
  100.7 10.7 %collective-permute-start.20 = (bf16[128,768]{1,0:T(8,128)(2,1)S(1)}, bf16[128,768]{1,0:T(8,128)(2,1)S(1)}, u32[]{:S(2)}, u32[]{:S(2)}) collective-permute-start(bf16[128,768]{1,0:T(8,128)(2,1)S(1)} %get-tuple-element.67), channel_id=1, source_target_pairs={{0,4},{1,5},{2,6},{3,7},{4,0},{5,1},{6,2},{7,3},{8,12},{9,13},{10,... | collective-permute-start | bytes 589832 | tf_op jit(solution)/shard_map/ppermute | solution.py:24
  128.6 25.6 %collective-permute-start.60 = (bf16[48,1536]{1,0:T(8,128)(2,1)S(1)}, bf16[48,1536]{1,0:T(8,128)(2,1)S(1)}, u32[]{:S(2)}, u32[]{:S(2)}) collective-permute-start(bf16[48,1536]{1,0:T(8,128)(2,1)S(1)} %get-tuple-element.18), channel_id=1, source_target_pairs={{0,32},{8,40},{16,48},{24,56},{32,64},{40,72},{48,80},{56,88},{64,... | collective-permute-start | bytes 442376 | tf_op jit(solution)/shard_map/ppermute | solution.py:20
  128.7 31.1 %collective-permute-start.59 = (bf16[48,1536]{1,0:T(8,128)(2,1)S(1)}, bf16[48,1536]{1,0:T(8,128)(2,1)S(1)}, u32[]{:S(2)}, u32[]{:S(2)}) collective-permute-start(bf16[48,1536]{1,0:T(8,128)(2,1)S(1)} %get-tuple-element.18), channel_id=1, source_target_pairs={{0,96},{8,104},{16,112},{24,120},{32,0},{40,8},{48,16},{56,24},{64... | collective-permute-start | bytes 442376 | tf_op jit(solution)/shard_map/ppermute | solution.py:20
  131.7 23.9 %collective-permute-start.31 = (bf16[48,1536]{1,0:T(8,128)(2,1)S(1)}, bf16[48,1536]{1,0:T(8,128)(2,1)S(1)}, u32[]{:S(2)}, u32[]{:S(2)}) collective-permute-start(bf16[48,1536]{1,0:T(8,128)(2,1)S(1)} %get-tuple-element.104), channel_id=1, source_target_pairs={{0,32},{8,40},{16,48},{24,56},{32,64},{40,72},{48,80},{56,88},{64,... | collective-permute-start | bytes 442376 | tf_op jit(solution)/shard_map/ppermute | solution.py:20
  131.7 29.1 %collective-permute-start.30 = (bf16[48,1536]{1,0:T(8,128)(2,1)S(1)}, bf16[48,1536]{1,0:T(8,128)(2,1)S(1)}, u32[]{:S(2)}, u32[]{:S(2)}) collective-permute-start(bf16[48,1536]{1,0:T(8,128)(2,1)S(1)} %get-tuple-element.104), channel_id=1, source_target_pairs={{0,96},{8,104},{16,112},{24,120},{32,0},{40,8},{48,16},{56,24},{64... | collective-permute-start | bytes 442376 | tf_op jit(solution)/shard_map/ppermute | solution.py:20
  134.4 18.3 %collective-permute-start.23 = (bf16[48,1536]{1,0:T(8,128)(2,1)S(1)}, bf16[48,1536]{1,0:T(8,128)(2,1)S(1)}, u32[]{:S(2)}, u32[]{:S(2)}) collective-permute-start(bf16[48,1536]{1,0:T(8,128)(2,1)S(1)} %get-tuple-element.108), channel_id=1, source_target_pairs={{0,8},{8,16},{16,24},{24,0},{32,40},{40,48},{48,56},{56,32},{64,72... | collective-permute-start | bytes 442376 | tf_op jit(solution)/shard_map/ppermute | solution.py:16
  152.7 9.9 %collective-permute-start.56 = (bf16[48,1536]{1,0:T(8,128)(2,1)S(1)}, bf16[48,1536]{1,0:T(8,128)(2,1)S(1)}, u32[]{:S(2)}, u32[]{:S(2)}) collective-permute-start(bf16[48,1536]{1,0:T(8,128)(2,1)S(1)} %get-tuple-element.106), channel_id=1, source_target_pairs={{0,24},{8,0},{16,8},{24,16},{32,56},{40,32},{48,40},{56,48},{64,88... | collective-permute-start | bytes 442376 | tf_op jit(solution)/shard_map/ppermute | solution.py:16
  159.7 18.1 %collective-permute-start.61 = (bf16[24,1536]{1,0:T(8,128)(2,1)S(1)}, bf16[24,1536]{1,0:T(8,128)(2,1)S(1)}, u32[]{:S(2)}, u32[]{:S(2)}) collective-permute-start(bf16[24,1536]{1,0:T(8,128)(2,1)S(1)} %slice.697), channel_id=1, source_target_pairs={{0,32},{8,40},{16,48},{24,56},{32,64},{40,72},{48,80},{56,88},{64,... | collective-permute-start | bytes 221192 | tf_op jit(solution)/shard_map/ppermute | solution.py:20
  160.9 20.2 %collective-permute-start.62 = (bf16[24,1536]{1,0:T(8,128)(2,1)S(1)}, bf16[24,1536]{1,0:T(8,128)(2,1)S(1)}, u32[]{:S(2)}, u32[]{:S(2)}) collective-permute-start(bf16[24,1536]{1,0:T(8,128)(2,1)S(1)} %slice.698), channel_id=1, source_target_pairs={{0,96},{8,104},{16,112},{24,120},{32,0},{40,8},{48,16},{56,24},{64... | collective-permute-start | bytes 221192 | tf_op jit(solution)/shard_map/ppermute | solution.py:20
  162.6 20.3 %collective-permute-start.32 = (bf16[24,1536]{1,0:T(8,128)(2,1)S(1)}, bf16[24,1536]{1,0:T(8,128)(2,1)S(1)}, u32[]{:S(2)}, u32[]{:S(2)}) collective-permute-start(bf16[24,1536]{1,0:T(8,128)(2,1)S(1)} %slice.669), channel_id=1, source_target_pairs={{0,32},{8,40},{16,48},{24,56},{32,64},{40,72},{48,80},{56,88},{64,... | collective-permute-start | bytes 221192 | tf_op jit(solution)/shard_map/ppermute | solution.py:20
  162.7 21.2 %collective-permute-start.33 = (bf16[24,1536]{1,0:T(8,128)(2,1)S(1)}, bf16[24,1536]{1,0:T(8,128)(2,1)S(1)}, u32[]{:S(2)}, u32[]{:S(2)}) collective-permute-start(bf16[24,1536]{1,0:T(8,128)(2,1)S(1)} %slice.670), channel_id=1, source_target_pairs={{0,96},{8,104},{16,112},{24,120},{32,0},{40,8},{48,16},{56,24},{64... | collective-permute-start | bytes 221192 | tf_op jit(solution)/shard_map/ppermute | solution.py:20
  177.6 25.9 %collective-permute-start.37 = (bf16[192,1536]{1,0:T(8,128)(2,1)}, bf16[192,1536]{1,0:T(8,128)(2,1)S(1)}, u32[]{:S(2)}, u32[]{:S(2)}) collective-permute-start(bf16[192,1536]{1,0:T(8,128)(2,1)} %constant_dynamic-update-slice_fusion.12), channel_id=1, source_target_pairs={{0,32},{8,40},{16,48},{24,56},{32,64},{40,72},{48,80},{56,88},{64,... | collective-permute-start | bytes 1769480 | tf_op jit(solution)/shard_map/ppermute | solution.py:20
  177.8 20.7 %collective-permute-start.27 = (bf16[192,1536]{1,0:T(8,128)(2,1)}, bf16[192,1536]{1,0:T(8,128)(2,1)S(1)}, u32[]{:S(2)}, u32[]{:S(2)}) collective-permute-start(bf16[192,1536]{1,0:T(8,128)(2,1)} %constant_dynamic-update-slice_fusion.12), channel_id=1, source_target_pairs={{0,96},{8,104},{16,112},{24,120},{32,0},{40,8},{48,16},{56,24},{64... | collective-permute-start | bytes 1769480 | tf_op jit(solution)/shard_map/ppermute | solution.py:20
  181.1 12.8 %collective-permute-start.58 = (bf16[192,1536]{1,0:T(8,128)(2,1)}, bf16[192,1536]{1,0:T(8,128)(2,1)S(1)}, u32[]{:S(2)}, u32[]{:S(2)}) collective-permute-start(bf16[192,1536]{1,0:T(8,128)(2,1)} %copy-done.42), channel_id=1, source_target_pairs={{0,96},{8,104},{16,112},{24,120},{32,0},{40,8},{48,16},{56,24},{64... | collective-permute-start | bytes 1769480 | tf_op jit(solution)/shard_map/ppermute | solution.py:20
  182.9 22.8 %collective-permute-start.66 = (bf16[192,1536]{1,0:T(8,128)(2,1)}, bf16[192,1536]{1,0:T(8,128)(2,1)S(1)}, u32[]{:S(2)}, u32[]{:S(2)}) collective-permute-start(bf16[192,1536]{1,0:T(8,128)(2,1)} %copy-done.42), channel_id=1, source_target_pairs={{0,32},{8,40},{16,48},{24,56},{32,64},{40,72},{48,80},{56,88},{64,... | collective-permute-start | bytes 1769480 | tf_op jit(solution)/shard_map/ppermute | solution.py:20
  195.5 11.3 %collective-permute-start.64 = (bf16[192,1536]{1,0:T(8,128)(2,1)}, bf16[192,1536]{1,0:T(8,128)(2,1)}, u32[]{:S(2)}, u32[]{:S(2)}) collective-permute-start(bf16[192,1536]{1,0:T(8,128)(2,1)} %get-tuple-element.87), channel_id=1, source_target_pairs={{0,24},{8,0},{16,8},{24,16},{32,56},{40,32},{48,40},{56,48},{64,88... | collective-permute-start | bytes 1769480 | tf_op jit(solution)/shard_map/ppermute | solution.py:16
  198.5 11.4 %collective-permute-start.63 = (bf16[192,1536]{1,0:T(8,128)(2,1)}, bf16[192,1536]{1,0:T(8,128)(2,1)}, u32[]{:S(2)}, u32[]{:S(2)}) collective-permute-start(bf16[192,1536]{1,0:T(8,128)(2,1)} %get-tuple-element.87), channel_id=1, source_target_pairs={{0,8},{8,16},{16,24},{24,0},{32,40},{40,48},{48,56},{56,32},{64,72... | collective-permute-start | bytes 1769480 | tf_op jit(solution)/shard_map/ppermute | solution.py:16
  200.2 11.8 %collective-permute-start.35 = (bf16[192,1536]{1,0:T(8,128)(2,1)}, bf16[192,1536]{1,0:T(8,128)(2,1)S(1)}, u32[]{:S(2)}, u32[]{:S(2)}) collective-permute-start(bf16[192,1536]{1,0:T(8,128)(2,1)} %get-tuple-element.97), channel_id=1, source_target_pairs={{0,24},{8,0},{16,8},{24,16},{32,56},{40,32},{48,40},{56,48},{64,88... | collective-permute-start | bytes 1769480 | tf_op jit(solution)/shard_map/ppermute | solution.py:16
  203.5 13.1 %collective-permute-start.34 = (bf16[192,1536]{1,0:T(8,128)(2,1)}, bf16[192,1536]{1,0:T(8,128)(2,1)}, u32[]{:S(2)}, u32[]{:S(2)}) collective-permute-start(bf16[192,1536]{1,0:T(8,128)(2,1)} %get-tuple-element.97), channel_id=1, source_target_pairs={{0,8},{8,16},{16,24},{24,0},{32,40},{40,48},{48,56},{56,32},{64,72... | collective-permute-start | bytes 1769480 | tf_op jit(solution)/shard_map/ppermute | solution.py:16
  205.8 87.9 %collective-permute-start.38 = (bf16[96,1536]{1,0:T(8,128)(2,1)S(1)}, bf16[96,1536]{1,0:T(8,128)(2,1)S(1)}, u32[]{:S(2)}, u32[]{:S(2)}) collective-permute-start(bf16[96,1536]{1,0:T(8,128)(2,1)S(1)} %slice.675), channel_id=1, source_target_pairs={{0,32},{8,40},{16,48},{24,56},{32,64},{40,72},{48,80},{56,88},{64,... | collective-permute-start | bytes 884744 | tf_op jit(solution)/shard_map/ppermute | solution.py:20
  206.8 86.8 %collective-permute-start.39 = (bf16[96,1536]{1,0:T(8,128)(2,1)S(1)}, bf16[96,1536]{1,0:T(8,128)(2,1)S(1)}, u32[]{:S(2)}, u32[]{:S(2)}) collective-permute-start(bf16[96,1536]{1,0:T(8,128)(2,1)S(1)} %slice.676), channel_id=1, source_target_pairs={{0,96},{8,104},{16,112},{24,120},{32,0},{40,8},{48,16},{56,24},{64... | collective-permute-start | bytes 884744 | tf_op jit(solution)/shard_map/ppermute | solution.py:20
  210.0 19.0 %collective-permute-start.67 = (bf16[96,1536]{1,0:T(8,128)(2,1)S(1)}, bf16[96,1536]{1,0:T(8,128)(2,1)S(1)}, u32[]{:S(2)}, u32[]{:S(2)}) collective-permute-start(bf16[96,1536]{1,0:T(8,128)(2,1)S(1)} %slice.703), channel_id=1, source_target_pairs={{0,32},{8,40},{16,48},{24,56},{32,64},{40,72},{48,80},{56,88},{64,... | collective-permute-start | bytes 884744 | tf_op jit(solution)/shard_map/ppermute | solution.py:20
  212.0 21.1 %collective-permute-start.68 = (bf16[96,1536]{1,0:T(8,128)(2,1)S(1)}, bf16[96,1536]{1,0:T(8,128)(2,1)S(1)}, u32[]{:S(2)}, u32[]{:S(2)}) collective-permute-start(bf16[96,1536]{1,0:T(8,128)(2,1)S(1)} %slice.704), channel_id=1, source_target_pairs={{0,96},{8,104},{16,112},{24,120},{32,0},{40,8},{48,16},{56,24},{64... | collective-permute-start | bytes 884744 | tf_op jit(solution)/shard_map/ppermute | solution.py:20
  216.6 9.9 %collective-permute-start.65 = (bf16[96,1536]{1,0:T(8,128)(2,1)S(1)}, bf16[96,1536]{1,0:T(8,128)(2,1)S(1)}, u32[]{:S(2)}, u32[]{:S(2)}) collective-permute-start(bf16[96,1536]{1,0:T(8,128)(2,1)S(1)} %slice.700), channel_id=1, source_target_pairs={{0,24},{8,0},{16,8},{24,16},{32,56},{40,32},{48,40},{56,48},{64,88... | collective-permute-start | bytes 884744 | tf_op jit(solution)/shard_map/ppermute | solution.py:16
  226.5 17.5 %collective-permute-start.69 = (bf16[96,1536]{1,0:T(8,128)(2,1)S(1)}, bf16[96,1536]{1,0:T(8,128)(2,1)S(1)}, u32[]{:S(2)}, u32[]{:S(2)}) collective-permute-start(bf16[96,1536]{1,0:T(8,128)(2,1)S(1)} %slice.709), channel_id=1, source_target_pairs={{0,8},{8,16},{16,24},{24,0},{32,40},{40,48},{48,56},{56,32},{64,72... | collective-permute-start | bytes 884744 | tf_op jit(solution)/shard_map/ppermute | solution.py:16
  228.9 64.4 %collective-permute-start.36 = (bf16[96,1536]{1,0:T(8,128)(2,1)S(1)}, bf16[96,1536]{1,0:T(8,128)(2,1)S(1)}, u32[]{:S(2)}, u32[]{:S(2)}) collective-permute-start(bf16[96,1536]{1,0:T(8,128)(2,1)S(1)} %slice.672), channel_id=1, source_target_pairs={{0,24},{8,0},{16,8},{24,16},{32,56},{40,32},{48,40},{56,48},{64,88... | collective-permute-start | bytes 884744 | tf_op jit(solution)/shard_map/ppermute | solution.py:16
  233.1 62.9 %collective-permute-start.40 = (bf16[96,1536]{1,0:T(8,128)(2,1)S(1)}, bf16[96,1536]{1,0:T(8,128)(2,1)S(1)}, u32[]{:S(2)}, u32[]{:S(2)}) collective-permute-start(bf16[96,1536]{1,0:T(8,128)(2,1)S(1)} %slice.681), channel_id=1, source_target_pairs={{0,8},{8,16},{16,24},{24,0},{32,40},{40,48},{48,56},{56,32},{64,72... | collective-permute-start | bytes 884744 | tf_op jit(solution)/shard_map/ppermute | solution.py:16
  312.5 13.8 %collective-permute-start.70 = (bf16[24,6144]{1,0:T(8,128)(2,1)S(1)}, bf16[24,6144]{1,0:T(8,128)(2,1)S(1)}, u32[]{:S(2)}, u32[]{:S(2)}) collective-permute-start(bf16[24,6144]{1,0:T(8,128)(2,1)S(1)} %get-tuple-element.29), channel_id=1, source_target_pairs={{0,8},{8,16},{16,24},{24,0},{32,40},{40,48},{48,56},{56,32},{64,72... | collective-permute-start | bytes 884744 | tf_op jit(solution)/shard_map/ppermute | solution.py:16
  313.4 15.7 %collective-permute-start.72 = (bf16[24,6144]{1,0:T(8,128)(2,1)S(1)}, bf16[24,6144]{1,0:T(8,128)(2,1)S(1)}, u32[]{:S(2)}, u32[]{:S(2)}) collective-permute-start(bf16[24,6144]{1,0:T(8,128)(2,1)S(1)} %get-tuple-element.30), channel_id=1, source_target_pairs={{0,24},{8,0},{16,8},{24,16},{32,56},{40,32},{48,40},{56,48},{64,88... | collective-permute-start | bytes 884744 | tf_op jit(solution)/shard_map/ppermute | solution.py:16
  323.6 8.5 %collective-permute-start.82 = (bf16[96,1536]{1,0:T(8,128)(2,1)S(1)}, bf16[96,1536]{1,0:T(8,128)(2,1)S(1)}, u32[]{:S(2)}, u32[]{:S(2)}) collective-permute-start(bf16[96,1536]{1,0:T(8,128)(2,1)S(1)} %get-tuple-element.49), channel_id=1, source_target_pairs={{0,96},{8,104},{16,112},{24,120},{32,0},{40,8},{48,16},{56,24},{64... | collective-permute-start | bytes 884744 | tf_op jit(solution)/shard_map/ppermute | solution.py:20
  326.3 7.5 %collective-permute-start.92 = (bf16[24,6144]{1,0:T(8,128)(2,1)S(1)}, bf16[24,6144]{1,0:T(8,128)(2,1)S(1)}, u32[]{:S(2)}, u32[]{:S(2)}) collective-permute-start(bf16[24,6144]{1,0:T(8,128)(2,1)S(1)} %get-tuple-element.36), channel_id=1, source_target_pairs={{0,24},{8,0},{16,8},{24,16},{32,56},{40,32},{48,40},{56,48},{64,88... | collective-permute-start | bytes 884744 | tf_op jit(solution)/shard_map/ppermute | solution.py:16
  332.1 10.8 %collective-permute-start.73 = (bf16[48,6144]{1,0:T(8,128)(2,1)S(1)}, bf16[48,6144]{1,0:T(8,128)(2,1)S(1)}, u32[]{:S(2)}, u32[]{:S(2)}) collective-permute-start(bf16[48,6144]{1,0:T(8,128)(2,1)S(1)} %pad_maximum_fusion.4), channel_id=1, source_target_pairs={{0,24},{8,0},{16,8},{24,16},{32,56},{40,32},{48,40},{56,48},{64,88... | collective-permute-start | bytes 1769480 | tf_op jit(solution)/shard_map/ppermute | solution.py:16
  333.0 9.9 %collective-permute-start.71 = (bf16[48,6144]{1,0:T(8,128)(2,1)S(1)}, bf16[48,6144]{1,0:T(8,128)(2,1)S(1)}, u32[]{:S(2)}, u32[]{:S(2)}) collective-permute-start(bf16[48,6144]{1,0:T(8,128)(2,1)S(1)} %pad_maximum_fusion.3), channel_id=1, source_target_pairs={{0,8},{8,16},{16,24},{24,0},{32,40},{40,48},{48,56},{56,32},{64,72... | collective-permute-start | bytes 1769480 | tf_op jit(solution)/shard_map/ppermute | solution.py:16
  333.8 11.1 %collective-permute-start.83 = (bf16[192,1536]{1,0:T(8,128)(2,1)S(1)}, bf16[192,1536]{1,0:T(8,128)(2,1)S(1)}, u32[]{:S(2)}, u32[]{:S(2)}) collective-permute-start(bf16[192,1536]{1,0:T(8,128)(2,1)S(1)} %pad_maximum_fusion.6), channel_id=1, source_target_pairs={{0,96},{8,104},{16,112},{24,120},{32,0},{40,8},{48,16},{56,24},{64... | collective-permute-start | bytes 1769480 | tf_op jit(solution)/shard_map/ppermute | solution.py:20
  336.1 11.7 %collective-permute-start.81 = (bf16[192,1536]{1,0:T(8,128)(2,1)S(1)}, bf16[192,1536]{1,0:T(8,128)(2,1)S(1)}, u32[]{:S(2)}, u32[]{:S(2)}) collective-permute-start(bf16[192,1536]{1,0:T(8,128)(2,1)S(1)} %pad_maximum_fusion.5), channel_id=1, source_target_pairs={{0,32},{8,40},{16,48},{24,56},{32,64},{40,72},{48,80},{56,88},{64,... | collective-permute-start | bytes 1769480 | tf_op jit(solution)/shard_map/ppermute | solution.py:20
  336.2 15.5 %collective-permute-start.93 = (bf16[48,6144]{1,0:T(8,128)(2,1)S(1)}, bf16[48,6144]{1,0:T(8,128)(2,1)S(1)}, u32[]{:S(2)}, u32[]{:S(2)}) collective-permute-start(bf16[48,6144]{1,0:T(8,128)(2,1)S(1)} %pad_maximum_fusion.8), channel_id=1, source_target_pairs={{0,24},{8,0},{16,8},{24,16},{32,56},{40,32},{48,40},{56,48},{64,88... | collective-permute-start | bytes 1769480 | tf_op jit(solution)/shard_map/ppermute | solution.py:16
  342.9 13.4 %collective-permute-start.91 = (bf16[48,6144]{1,0:T(8,128)(2,1)S(1)}, bf16[48,6144]{1,0:T(8,128)(2,1)S(1)}, u32[]{:S(2)}, u32[]{:S(2)}) collective-permute-start(bf16[48,6144]{1,0:T(8,128)(2,1)S(1)} %pad_maximum_fusion.7), channel_id=1, source_target_pairs={{0,8},{8,16},{16,24},{24,0},{32,40},{40,48},{48,56},{56,32},{64,72... | collective-permute-start | bytes 1769480 | tf_op jit(solution)/shard_map/ppermute | solution.py:16
  342.9 13.8 %collective-permute-start.48 = (bf16[192,1536]{1,0:T(8,128)(2,1)S(1)}, bf16[192,1536]{1,0:T(8,128)(2,1)S(1)}, u32[]{:S(2)}, u32[]{:S(2)}) collective-permute-start(bf16[192,1536]{1,0:T(8,128)(2,1)S(1)} %pad_maximum_fusion.2), channel_id=1, source_target_pairs={{0,96},{8,104},{16,112},{24,120},{32,0},{40,8},{48,16},{56,24},{64... | collective-permute-start | bytes 1769480 | tf_op jit(solution)/shard_map/ppermute | solution.py:20
  344.9 14.6 %collective-permute-start.46 = (bf16[192,1536]{1,0:T(8,128)(2,1)S(1)}, bf16[192,1536]{1,0:T(8,128)(2,1)S(1)}, u32[]{:S(2)}, u32[]{:S(2)}) collective-permute-start(bf16[192,1536]{1,0:T(8,128)(2,1)S(1)} %pad_maximum_fusion.1), channel_id=1, source_target_pairs={{0,32},{8,40},{16,48},{24,56},{32,64},{40,72},{48,80},{56,88},{64,... | collective-permute-start | bytes 1769480 | tf_op jit(solution)/shard_map/ppermute | solution.py:20
  347.9 12.1 %collective-permute-start.74 = (bf16[24,1536]{1,0:T(8,128)(2,1)S(1)}, bf16[24,1536]{1,0:T(8,128)(2,1)S(1)}, u32[]{:S(2)}, u32[]{:S(2)}) collective-permute-start(bf16[24,1536]{1,0:T(8,128)(2,1)S(1)} %get-tuple-element.83), channel_id=1, source_target_pairs={{0,32},{8,40},{16,48},{24,56},{32,64},{40,72},{48,80},{56,88},{64,... | collective-permute-start | bytes 221192 | tf_op jit(solution)/shard_map/ppermute | solution.py:20
  351.7 10.9 %collective-permute-start.76 = (bf16[24,1536]{1,0:T(8,128)(2,1)S(1)}, bf16[24,1536]{1,0:T(8,128)(2,1)S(1)}, u32[]{:S(2)}, u32[]{:S(2)}) collective-permute-start(bf16[24,1536]{1,0:T(8,128)(2,1)S(1)} %get-tuple-element.84), channel_id=1, source_target_pairs={{0,96},{8,104},{16,112},{24,120},{32,0},{40,8},{48,16},{56,24},{64... | collective-permute-start | bytes 221192 | tf_op jit(solution)/shard_map/ppermute | solution.py:20
  356.7 9.0 %collective-permute-start.86 = (bf16[24,1536]{1,0:T(8,128)(2,1)S(1)}, bf16[24,1536]{1,0:T(8,128)(2,1)S(1)}, u32[]{:S(2)}, u32[]{:S(2)}) collective-permute-start(bf16[24,1536]{1,0:T(8,128)(2,1)S(1)} %get-tuple-element.73), channel_id=1, source_target_pairs={{0,24},{8,0},{16,8},{24,16},{32,56},{40,32},{48,40},{56,48},{64,88... | collective-permute-start | bytes 221192 | tf_op jit(solution)/shard_map/ppermute | solution.py:16
  359.9 7.4 %collective-permute-start.96 = (bf16[24,1536]{1,0:T(8,128)(2,1)S(1)}, bf16[24,1536]{1,0:T(8,128)(2,1)S(1)}, u32[]{:S(2)}, u32[]{:S(2)}) collective-permute-start(bf16[24,1536]{1,0:T(8,128)(2,1)S(1)} %get-tuple-element.92), channel_id=1, source_target_pairs={{0,96},{8,104},{16,112},{24,120},{32,0},{40,8},{48,16},{56,24},{64... | collective-permute-start | bytes 221192 | tf_op jit(solution)/shard_map/ppermute | solution.py:20
  370.6 28.7 %collective-permute-start.95 = (bf16[48,1536]{1,0:T(8,128)(2,1)S(1)}, bf16[48,1536]{1,0:T(8,128)(2,1)S(1)}, u32[]{:S(2)}, u32[]{:S(2)}) collective-permute-start(bf16[48,1536]{1,0:T(8,128)(2,1)S(1)} %pad_maximum_fusion.19), channel_id=1, source_target_pairs={{0,32},{8,40},{16,48},{24,56},{32,64},{40,72},{48,80},{56,88},{64,... | collective-permute-start | bytes 442376 | tf_op jit(solution)/shard_map/ppermute | solution.py:20
  371.7 29.3 %collective-permute-start.52 = (bf16[48,1536]{1,0:T(8,128)(2,1)S(1)}, bf16[48,1536]{1,0:T(8,128)(2,1)S(1)}, u32[]{:S(2)}, u32[]{:S(2)}) collective-permute-start(bf16[48,1536]{1,0:T(8,128)(2,1)S(1)} %pad_maximum_fusion.14), channel_id=1, source_target_pairs={{0,24},{8,0},{16,8},{24,16},{32,56},{40,32},{48,40},{56,48},{64,88... | collective-permute-start | bytes 442376 | tf_op jit(solution)/shard_map/ppermute | solution.py:16
  373.0 31.0 %collective-permute-start.50 = (bf16[48,1536]{1,0:T(8,128)(2,1)S(1)}, bf16[48,1536]{1,0:T(8,128)(2,1)S(1)}, u32[]{:S(2)}, u32[]{:S(2)}) collective-permute-start(bf16[48,1536]{1,0:T(8,128)(2,1)S(1)} %pad_maximum_fusion.13), channel_id=1, source_target_pairs={{0,8},{8,16},{16,24},{24,0},{32,40},{40,48},{48,56},{56,32},{64,72... | collective-permute-start | bytes 442376 | tf_op jit(solution)/shard_map/ppermute | solution.py:16
  375.0 30.0 %collective-permute-start.78 = (bf16[48,768]{1,0:T(8,128)(2,1)S(1)}, bf16[48,768]{1,0:T(8,128)(2,1)S(1)}, u32[]{:S(2)}, u32[]{:S(2)}) collective-permute-start(bf16[48,768]{1,0:T(8,128)(2,1)S(1)} %get-tuple-element.81), channel_id=1, source_target_pairs={{0,2},{1,3},{2,4},{3,5},{4,6},{5,7},{6,0},{7,1},{8,10},{9,11},{10,... | collective-permute-start | bytes 221192 | tf_op jit(solution)/shard_map/ppermute | solution.py:24
  375.4 29.2 %collective-permute-start.79 = (bf16[48,768]{1,0:T(8,128)(2,1)S(1)}, bf16[48,768]{1,0:T(8,128)(2,1)S(1)}, u32[]{:S(2)}, u32[]{:S(2)}) collective-permute-start(bf16[48,768]{1,0:T(8,128)(2,1)S(1)} %get-tuple-element.82), channel_id=1, source_target_pairs={{0,3},{1,2},{2,5},{3,4},{4,7},{5,6},{6,1},{7,0},{8,11},{9,10},{10,... | collective-permute-start | bytes 221192 | tf_op jit(solution)/shard_map/ppermute | solution.py:24
  399.3 8.5 %collective-permute-start.88 = (bf16[48,768]{1,0:T(8,128)(2,1)S(1)}, bf16[48,768]{1,0:T(8,128)(2,1)S(1)}, u32[]{:S(2)}, u32[]{:S(2)}) collective-permute-start(bf16[48,768]{1,0:T(8,128)(2,1)S(1)} %get-tuple-element.85), channel_id=1, source_target_pairs={{0,4},{1,5},{2,6},{3,7},{4,0},{5,1},{6,2},{7,3},{8,12},{9,13},{10,... | collective-permute-start | bytes 221192 | tf_op jit(solution)/shard_map/ppermute | solution.py:24
  404.0 7.3 %collective-permute-start.98 = (bf16[48,768]{1,0:T(8,128)(2,1)S(1)}, bf16[48,768]{1,0:T(8,128)(2,1)S(1)}, u32[]{:S(2)}, u32[]{:S(2)}) collective-permute-start(bf16[48,768]{1,0:T(8,128)(2,1)S(1)} %get-tuple-element.89), channel_id=1, source_target_pairs={{0,6},{1,7},{2,0},{3,1},{4,2},{5,3},{6,4},{7,5},{8,14},{9,15},{10,... | collective-permute-start | bytes 221192 | tf_op jit(solution)/shard_map/ppermute | solution.py:24
  413.1 15.8 %collective-permute-start.100 = (bf16[128,768]{1,0:T(8,128)(2,1)S(1)}, bf16[128,768]{1,0:T(8,128)(2,1)S(1)}, u32[]{:S(2)}, u32[]{:S(2)}) collective-permute-start(bf16[128,768]{1,0:T(8,128)(2,1)S(1)} %add_convert_fusion.8), channel_id=1, source_target_pairs={{0,0},{1,1},{2,32},{3,33},{4,64},{5,65},{6,96},{7,97},{8,8},{9,9},... | collective-permute-start | bytes 589832 | tf_op jit(solution)/shard_map/ppermute | solution.py:34
  (98 other events, 2199.3 us)
